TPU v7x, 32 devices: a whole 2x2x4 slice. The times are simulated.
32 devices in a mesh: epoch: 2 (over x), tile: 16 (over z, y, core).
Axes of the slice: x: 2, y: 2, z: 4, core: 2. Of those that a mesh axis runs over, the one named last changes fastest.
Arguments:
- owners: int32 [2, 2048], P('epoch', 'tile'), may hold values from 0 to 15, as said below
- row_offsets: int32 [2, 2048], P('epoch', 'tile'), may hold values from 0 to 224
- col_offsets: int32 [2, 2048], P('epoch', 'tile'), may hold values from 0 to 4064
- samples: bfloat16 [2, 2048, 2, 256], P('epoch', 'tile'), may hold values from -6 to 6
- coords: float32 [2, 2048, 2, 256], P('epoch', 'tile'), may hold values from 4 to 28
- taper_rows: float32 [16, 256], P('epoch'), may hold values from 1 to 4
- taper_cols: float32 [4096], P('tile'), may hold values from 1 to 4
Outputs:
- image: float32 [16, 256, 4096], P('epoch', None, 'tile')
Inputs may be any that keep to these rules, and one draw needn't show every extreme that they name: `owners`: in every epoch, within each aligned block of 128 slots (the slots of one index of tile), no owner tile is named more than 10 times, and one owner tile is named exactly 10 times in every block of that epoch.
All inputs are finite; a program needn't handle non-finite values.
Results may differ from a plain program's by a relative error of at most 0.0053.
Values may be sent and summed in bfloat16 or wider, within the bound.
A program may use at most 128 MiB of HBM per device.

v0:
```python
import functools
import math

import jax
import jax.numpy as jnp
import numpy as np
from jax import lax
from jax.experimental import pallas as pl
from jax.experimental.pallas import tpu as pltpu
from jax.sharding import PartitionSpec as P

SUB = 32
LANES = 128
EDGE = 16
FIELDS = 8
UNROLL = 8
BEHIND = 3
CUTS = 4
VMEM_BYTES = 24 * 1024 * 1024
MESH = pl.DeviceIdType.MESH


def dft(values, wanted, modulus=None):
    count = len(values)
    if all(v is None for v in values):
        return [None] * wanted
    if count == 1:
        return list(values)
    half = count // 2
    need = min(wanted, half)
    even, odd = dft(values[0::2], need), dft(values[1::2], need)
    low, high = [], []
    for k in range(need):
        e, o = even[k], odd[k]
        t = None if o is None else turn(o, k, count)
        low.append(plus(e, t))
        if half + k < wanted:
            high.append(minus(e, t))
    return low + high


def turn(value, k, count):
    re, im = value
    s = math.sqrt(0.5)
    k %= count
    if k == 0:
        return re, im
    if 2 * k == count:
        return -re, -im
    if 4 * k == count:
        return -im, re
    if 8 * k == count:
        return (re - im) * s, (re + im) * s
    if 8 * k == 3 * count:
        return (re + im) * -s, (re - im) * s
    c, s = math.cos(2 * math.pi * k / count), math.sin(2 * math.pi * k / count)
    return re * c - im * s, re * s + im * c


def plus(a, b):
    if a is None or b is None:
        return b if a is None else a
    return a[0] + b[0], a[1] + b[1]


def minus(a, b):
    if b is None:
        return a
    if a is None:
        return -b[0], -b[1]
    return a[0] - b[0], a[1] - b[1]


def epoch_turn(value, j, epoch, epoch_count):
    angles = [2 * math.pi * ((j * e) % epoch_count) / epoch_count for e in range(epoch_count)]

    def pick(numbers):
        chosen = jnp.float32(numbers[0])
        for e in range(1, epoch_count):
            chosen = jnp.where(epoch == e, jnp.float32(numbers[e]), chosen)
        return chosen

    cos, sin = [round(math.cos(a), 15) for a in angles], [round(math.sin(a), 15) for a in angles]
    re, im = value
    if not any(sin):
        if all(c == 1.0 for c in cos):
            return value
        c = pick(cos)
        return re * c, im * c
    c, s = pick(cos), pick(sin)
    return re * c - im * s, re * s + im * c


def exclusive(a, b, count):
    total = 0
    for bit in range(count.bit_length() - 1):
        x, y = lax.rem(a // (1 << bit), 2), lax.rem(b // (1 << bit), 2)
        total += (x + y - 2 * x * y) * (1 << bit)
    return total


def near_and_far(i, count):
    return jnp.where(
        i == count - 2,
        count - 1,
        jnp.where(lax.rem(i, 2) == 0, 1 + i // 2, count // 2 + i // 2),
    )


def grid_kernel(
    sizes,
    *refs,
):
    tile_count, epoch_count, capacity, band = sizes
    inputs, (pool_ref, list_ref, weight_ref), scratch = refs[:5], refs[5:8], refs[8:]
    owner_ref, row_ref, col_ref, coords_ref, samples_ref, in_sem = scratch[:6]
    packed, raw = scratch[6:8], scratch[8:10]
    t_send, t_recv, x_send, x_recv = scratch[10:]
    fetches = [
        pltpu.make_async_copy(given, held, in_sem.at[i])
        for i, (given, held) in enumerate(zip(inputs, scratch))
    ]
    for fetch in fetches:
        fetch.start()
    me, epoch = lax.axis_index("tile"), lax.axis_index("epoch")
    n_slots = owner_ref.shape[1]
    n_samples = coords_ref.shape[3]
    pieces = n_samples // LANES
    lane_step = max(FIELDS, 1 << (capacity - 1).bit_length())
    pad = -(-capacity // FIELDS) * FIELDS
    info = 2 * pieces * capacity
    info_rows = raw[1].shape[1] - info
    half = tile_count // 2
    per_meta = LANES // lane_step
    groups = -(-tile_count // per_meta)
    slot_rows = SUB // 2

    barrier = pltpu.get_barrier_semaphore()

    def greet(k, carry):
        peer = lax.rem(me + k, tile_count)
        pl.semaphore_signal(barrier, inc=1, device_id={"tile": peer}, device_id_type=MESH)
        return carry

    lax.fori_loop(1, tile_count, greet, 0)
    for k in range(1, epoch_count):
        peer = lax.rem(epoch + k, epoch_count)
        pl.semaphore_signal(barrier, inc=1, device_id={"epoch": peer}, device_id_type=MESH)

    for fetch in fetches:
        fetch.wait()
    owner = owner_ref[...]
    mirrored = owner >= half
    target = jnp.where(mirrored, 2 * (tile_count - 1 - owner) + 1, 2 * owner)
    row = jnp.where(mirrored, band - (SUB - 1) - row_ref[...], row_ref[...])
    col = jnp.where(mirrored, tile_count * band - (SUB - 1) - col_ref[...], col_ref[...])
    mine = lax.broadcasted_iota(jnp.int32, (tile_count, n_slots), 0) == target
    before = lax.broadcasted_iota(jnp.int32, (n_slots, n_slots), 0) < lax.broadcasted_iota(
        jnp.int32, (n_slots, n_slots), 1
    )
    rank = jnp.dot(
        jnp.where(mine, 1.0, 0.0).astype(jnp.bfloat16),
        jnp.where(before, 1.0, 0.0).astype(jnp.bfloat16),
        preferred_element_type=jnp.float32,
    ).astype(jnp.int32)
    key = jnp.where(mine, rank, -LANES)
    fields = [jnp.ones_like(row), row, col // LANES, col % LANES]
    fields = jnp.concatenate(fields + [jnp.zeros_like(row)] * (info_rows - len(fields)), 0)
    fields = fields.astype(jnp.float32).astype(jnp.bfloat16)
    lane = lax.broadcasted_iota(jnp.int32, (LANES, n_slots), 0) - lax.rem(me, per_meta) * lane_step
    first = lax.broadcasted_iota(jnp.int32, (pad, n_slots), 0)
    hits, notes = [], []
    for t in range(tile_count):
        hits.append(jnp.where(key[t : t + 1] == first, 1.0, 0.0))
        spot = jnp.where(key[t : t + 1] == lane, 1.0, 0.0).astype(jnp.bfloat16)
        notes.append(
            lax.dot_general(
                fields, spot, (((1,), (1,)), ((), ())), preferred_element_type=jnp.float32
            )
        )
    hits = jnp.concatenate(hits, 0)
    here = jnp.dot(
        hits,
        jnp.concatenate([coords_ref[0, :, p, :] for p in range(2)], 1) * 0.25,
        precision=lax.Precision.HIGHEST,
        preferred_element_type=jnp.float32,
    )
    samples = samples_ref[0].astype(jnp.float32)
    samples = jnp.concatenate([samples[:, p, :] for p in range(2)], 1).astype(jnp.bfloat16)
    values = jnp.dot(hits.astype(jnp.bfloat16), samples, preferred_element_type=jnp.float32)
    for t in range(tile_count):
        for part, block in enumerate((here, values)):
            rows = [
                block[t * pad : t * pad + capacity, q * LANES : (q + 1) * LANES]
                for q in range(2 * pieces)
            ]
            if part == 1:
                rows.append(notes[t])
            packed[part][t] = jnp.concatenate(rows, 0).astype(packed[part].dtype)
    pl.semaphore_wait(barrier, tile_count + epoch_count - 2)

    def tile_copies(k):
        peer = exclusive(me, k, tile_count)
        return [
            pltpu.make_async_remote_copy(
                src_ref=packed[part].at[peer],
                dst_ref=raw[part].at[me],
                send_sem=t_send.at[part, k],
                recv_sem=t_recv.at[part, k],
                device_id={"tile": peer},
                device_id_type=MESH,
            )
            for part in range(2)
        ]

    def epoch_copies(k, j):
        origin = exclusive(me, k, tile_count)
        return [
            pltpu.make_async_remote_copy(
                src_ref=raw[part].at[origin],
                dst_ref=raw[part].at[j * tile_count + origin],
                send_sem=x_send.at[part, (j - 1) * tile_count + k],
                recv_sem=x_recv.at[part, (j - 1) * tile_count + k],
                device_id={"epoch": lax.rem(epoch + j, epoch_count)},
                device_id_type=MESH,
            )
            for part in range(2)
        ]

    def send(i, carry):
        for copy in tile_copies(near_and_far(i, tile_count)):
            copy.start()
        return carry

    lax.fori_loop(0, tile_count - 1, send, 0)
    for part in range(2):
        raw[part][me] = packed[part][me]
    for j in range(1, epoch_count):
        for copy in epoch_copies(0, j):
            copy.start()

    flip = lax.rem(me, 2)
    cells = lax.broadcasted_iota(jnp.int32, (SUB, n_samples), 0)
    cells = jnp.where(flip == 1, SUB - 1 - cells, cells).astype(jnp.float32) * 0.25
    sign = (1 - 2 * flip).astype(jnp.float32)

    def weights(at):
        distance = cells - at
        return jnp.square(jnp.maximum(1.0 - distance * distance, 0.0))

    def make(at):
        points, values = raw[0][at], raw[1][at].astype(jnp.float32)

        def line(block, part, k):
            rows = [(part * pieces + q) * capacity + k for q in range(pieces)]
            return jnp.concatenate([block[row : row + 1] for row in rows], 1)

        for k in range(capacity):
            along_u = weights(line(points, 0, k)).astype(jnp.bfloat16)
            along_v = weights(line(points, 1, k))
            re = line(values, 0, k) * along_v
            im = (line(values, 1, k) * sign) * along_v
            subgrid = lax.dot_general(
                along_u,
                jnp.concatenate([re, im], 0).astype(jnp.bfloat16),
                (((1,), (1,)), ((), ())),
                preferred_element_type=jnp.float32,
            )
            pool_ref[at, k * slot_rows : (k + 1) * slot_rows, :] = jnp.concatenate(
                [subgrid[:slot_rows], subgrid[slot_rows:]], 1
            ).astype(jnp.bfloat16)

    make(me)

    def take(i):
        k = near_and_far(i, tile_count)
        for copy in tile_copies(k):
            copy.wait_recv()
        for j in range(1, epoch_count):
            for copy in epoch_copies(k, j):
                copy.start()
        make(exclusive(me, k, tile_count))

    def take_crossed(i):
        k = jnp.where(i == 0, 0, near_and_far(i - 1, tile_count))
        for j in range(1, epoch_count):
            for copy in epoch_copies(k, j):
                copy.wait_recv()
            make(j * tile_count + exclusive(me, k, tile_count))

    behind = min(BEHIND, tile_count - 1)

    def ahead(i, carry):
        take(i)
        return carry

    def both(i, carry):
        take(i)
        take_crossed(i - behind)
        return carry

    def crossed(i, carry):
        take_crossed(i)
        return carry

    lax.fori_loop(0, behind, ahead, 0)
    lax.fori_loop(behind, tile_count - 1, both, 0)

    rows_here = band // epoch_count
    first_row = (epoch * rows_here - SUB).astype(jnp.float32)
    spots = groups * LANES
    below = lax.broadcasted_iota(jnp.int32, (LANES, LANES), 0) < lax.broadcasted_iota(
        jnp.int32, (LANES, LANES), 1
    )
    below = jnp.where(below, 1.0, 0.0).astype(jnp.bfloat16)
    spot = lax.broadcasted_iota(jnp.int32, (spots, LANES), 0).astype(jnp.float32)
    lanes = lax.broadcasted_iota(jnp.int32, (1, LANES), 1)
    field = lax.broadcasted_iota(jnp.int32, (FIELDS, spots), 0)

    def list_slots(j):
        found, held = jnp.zeros((1, 1), jnp.float32), jnp.zeros((1, 1), jnp.float32)
        gathered = jnp.zeros((EDGE, spots), jnp.float32)
        for g in range(groups):
            total = jnp.zeros((info_rows, LANES), jnp.float32)
            for s in range(g * per_meta, min(tile_count, (g + 1) * per_meta)):
                total += raw[1][j * tile_count + s, info:, :].astype(jnp.float32)
            valid, row = total[0:1], total[1:2] - first_row
            inside = (valid > 0) & (row > 0) & (row < rows_here + SUB)
            mask = jnp.where(inside, 1.0, 0.0)
            order = jnp.dot(
                mask.astype(jnp.bfloat16), below, preferred_element_type=jnp.float32
            )
            chosen = spot == jnp.where(inside, order + found, -1.0)
            source = (g * per_meta + lanes // lane_step).astype(jnp.float32)
            place = (lanes % lane_step).astype(jnp.float32)
            rows = [source, row, total[2:3], total[3:4], place]
            rows = jnp.concatenate(rows + [jnp.zeros_like(row)] * (EDGE - len(rows)), 0)
            gathered += lax.dot_general(
                rows.astype(jnp.bfloat16),
                jnp.where(chosen, 1.0, 0.0).astype(jnp.bfloat16),
                (((1,), (1,)), ((), ())),
                preferred_element_type=jnp.float32,
            )
            found += jnp.sum(mask, 1, keepdims=True)
            held += jnp.sum(valid, 1, keepdims=True)
        listed = jnp.where(field == FIELDS - 1, found, gathered[:FIELDS])
        list_ref[j] = listed.astype(jnp.int32)
        weight_ref[j] = jnp.broadcast_to(1.0 / jnp.maximum(held, 1.0), (FIELDS, LANES))

    list_slots(0)
    lax.fori_loop(tile_count - 1 - behind, tile_count, crossed, 0)
    for j in range(1, epoch_count):
        list_slots(j)

    def finish(k, carry):
        for copy in tile_copies(k):
            copy.wait_send()
        return carry

    lax.fori_loop(1, tile_count, finish, 0)

    def settle(k, carry):
        for j in range(1, epoch_count):
            for copy in epoch_copies(k, j):
                copy.wait_send()
        return carry

    lax.fori_loop(0, tile_count, settle, 0)


def place_kernel(tile_count, list_ref, weight_ref, pool_ref, acc):
    acc_rows = acc.shape[2]
    slot_rows = SUB // 2

    def clear(i, carry):
        acc[0, i] = jnp.zeros((acc_rows, LANES), jnp.float32)
        acc[1, i] = jnp.zeros((acc_rows, LANES), jnp.float32)
        return carry

    lax.fori_loop(0, acc.shape[1], clear, 0)
    lanes = lax.broadcasted_iota(jnp.int32, (slot_rows, LANES), 1)

    for e in range(list_ref.shape[0]):
        weight = jnp.concatenate([weight_ref[e]] * (slot_rows // FIELDS), 0)

        def per_batch(b, carry, e=e, weight=weight):
            placed = []
            for k in range(UNROLL):
                at = b * UNROLL + k
                source, row, block, start, place = (list_ref[e, f, at] for f in range(5))
                first = pl.multiple_of(place * slot_rows, slot_rows)
                data = pool_ref[e * tile_count + source, pl.ds(first, slot_rows), :]
                data = data.astype(jnp.float32) * weight
                turned = [
                    pltpu.roll(data, lax.rem(start + (LANES - i * SUB), LANES), 1)
                    for i in range(4)
                ]
                near = (lanes >= start) & (lanes < start + SUB)
                far = lanes < start + SUB - LANES
                windows = [
                    jnp.concatenate([jnp.where(mask, turned[i], 0.0) for i in (p, 2 + p)], 0)
                    for p in range(2)
                    for mask in (near, far)
                ]
                placed.append((row, block, windows))
            for row, block, windows in placed:
                spots = [(p, block + h, pl.ds(row, SUB)) for p in range(2) for h in range(2)]
                sums = [acc[spot] + window for spot, window in zip(spots, windows)]
                for spot, total in zip(spots, sums):
                    acc[spot] = total
            return carry

        lax.fori_loop(0, (list_ref[e, FIELDS - 1, 0] + UNROLL - 1) // UNROLL, per_batch, 0)


def swap_kernel(
    sizes, cuts, acc_ref, cos_ref, sin_ref, second_ref, last_ref, mixed_ref, here_ref, *scratch
):
    tile_count, epoch_count, band = sizes
    table_sem, scratch = scratch[0], scratch[1:]
    turned, given, landed, folded, full = scratch[:5]
    p_send, p_recv, t_send, t_recv, x_send, x_recv = scratch[5:]
    me, epoch = lax.axis_index("tile"), lax.axis_index("epoch")
    half, kept = tile_count // 2, tile_count // epoch_count
    mine, side = me // 2, lax.rem(me, 2)
    partner = me + 1 - 2 * side
    table_copy = pltpu.make_async_copy(
        last_ref.at[pl.ds(epoch * kept, kept)], here_ref, table_sem.at[0]
    )
    table_copy.start()
    rows_here = band // epoch_count
    cut_rows = rows_here // cuts
    width = min(LANES, band)
    chunks = band // width
    parts = 2 * chunks
    lane_blocks = acc_ref.shape[1] - 1
    group = min(16, cut_rows)
    batch = min(8, half)

    barrier = pltpu.get_barrier_semaphore()

    def greet(k, carry):
        peer = exclusive(mine, k, half) * 2 + side
        pl.semaphore_signal(barrier, inc=1, device_id={"tile": peer}, device_id_type=MESH)
        return carry

    lax.fori_loop(1, half, greet, 0)
    pl.semaphore_signal(barrier, inc=1, device_id={"tile": partner}, device_id_type=MESH)
    for k in range(1, epoch_count):
        peer = lax.rem(epoch + k, epoch_count)
        pl.semaphore_signal(barrier, inc=1, device_id={"epoch": peer}, device_id_type=MESH)

    def rows_of(cut):
        edge = EDGE if cut == cuts - 1 else 0
        return pl.ds(cut * parts * cut_rows, parts * cut_rows + edge)

    def partner_copy(cut, k):
        return pltpu.make_async_remote_copy(
            src_ref=given.at[k, rows_of(cut)],
            dst_ref=landed.at[k, rows_of(cut)],
            send_sem=p_send.at[cut * half + k],
            recv_sem=p_recv.at[cut * half + k],
            device_id={"tile": partner},
            device_id_type=MESH,
        )

    def tile_copy(cut, k):
        return pltpu.make_async_remote_copy(
            src_ref=folded.at[k, rows_of(cut)],
            dst_ref=full.at[epoch * half + mine, rows_of(cut)],
            send_sem=t_send.at[cut * half + k],
            recv_sem=t_recv.at[cut * half + k],
            device_id={"tile": exclusive(mine, k, half) * 2 + side},
            device_id_type=MESH,
        )

    def epoch_copy(cut, k, j):
        origin = epoch * half + exclusive(mine, k, half)
        at = (cut * (epoch_count - 1) + j - 1) * half + k
        return pltpu.make_async_remote_copy(
            src_ref=full.at[origin, rows_of(cut)],
            dst_ref=full.at[origin, rows_of(cut)],
            send_sem=x_send.at[at],
            recv_sem=x_recv.at[at],
            device_id={"epoch": lax.rem(epoch + j, epoch_count)},
            device_id_type=MESH,
        )

    def transform(first, size):
        for h in range(chunks):
            values = []
            for a in range(tile_count):
                col = a * band + h * width
                lane, at = col % LANES, col // LANES
                value = [
                    acc_ref[p, at, pl.ds(SUB + first, size), lane : lane + width] for p in range(2)
                ]
                if col == 0:
                    for p in range(2):
                        value[p] += acc_ref[p, lane_blocks, pl.ds(SUB + first, size), :width]
                values.append(tuple(value))
            lanes = slice(h * width, (h + 1) * width)
            for m, (re, im) in enumerate(dft(values, tile_count)):
                c, s = cos_ref[m : m + 1, lanes], sin_ref[m : m + 1, lanes]
                pair = (re * c - im * s, re * s + im * c)
                for p in range(2):
                    start = p * band + h * width
                    turned[m, pl.ds(first, size), start : start + width] = pair[p].astype(
                        jnp.bfloat16
                    )

    edge_row = lax.broadcasted_iota(jnp.int32, (EDGE, width), 0)
    has_edge = jnp.where(epoch == epoch_count - 1, 1.0, 0.0)

    def sections(cut, tiles):
        rows = cut_rows + (EDGE if cut == cuts - 1 else 0)
        stack = [turned[tile, cut * cut_rows : cut * cut_rows + rows, :] for tile in tiles]
        moved = jnp.dot(
            jnp.concatenate(stack, 0), second_ref[...], preferred_element_type=jnp.float32
        )
        blocks = []
        for i in range(len(tiles)):
            pieces = [
                moved[i * rows : (i + 1) * rows, q * width : (q + 1) * width] for q in range(parts)
            ]
            block = [piece[:cut_rows] for piece in pieces]
            if cut == cuts - 1:
                edge = jnp.zeros((EDGE, width), jnp.float32)
                for q, piece in enumerate(pieces):
                    edge = jnp.where(edge_row == q, piece[cut_rows : cut_rows + 1] * has_edge, edge)
                block.append(edge)
            blocks.append(jnp.concatenate(block, 0))
        return blocks

    def forward(cut, k):
        tile_copy(cut, k).wait_recv()
        for j in range(1, epoch_count):
            epoch_copy(cut, k, j).start()

    order = [0] + [k for pair in zip(range(1, half), range(half // 2, half)) for k in pair]
    order = order[: 1 + 2 * (half // 2 - 1)] + [half - 1] if half > 1 else [0]
    pending = []
    for cut in range(cuts):

        def row_group(i, carry):
            transform(pl.multiple_of(i * group, group), group)
            return carry

        if not pending:
            steps = cut_rows // group
            lax.fori_loop(cut * steps, (cut + 1) * steps, row_group, 0)
        else:
            for i in range(cut_rows // group):
                transform(cut * cut_rows + i * group, group)
                if pending:
                    forward(*pending.pop(0))
        if cut == cuts - 1:
            transform(rows_here, EDGE)
        if cut == 0:
            pl.semaphore_wait(barrier, half + epoch_count - 1)
        for b in range(0, half, batch):
            ks = order[b : b + batch]
            tiles = [exclusive(mine, k, half) * 2 + 1 - side for k in ks]
            for k, block in zip(ks, sections(cut, tiles)):
                given[k, rows_of(cut), :] = block.astype(jnp.bfloat16)
                partner_copy(cut, k).start()
        for b in range(0, half, batch):
            ks = order[b : b + batch]
            tiles = [exclusive(mine, k, half) * 2 + side for k in ks]
            for k, block in zip(ks, sections(cut, tiles)):
                partner_copy(cut, k).wait_recv()
                both = (block + landed[k, rows_of(cut), :].astype(jnp.float32)).astype(jnp.bfloat16)
                if k == 0:
                    full[epoch * half + mine, rows_of(cut), :] = both
                    for j in range(1, epoch_count):
                        epoch_copy(cut, 0, j).start()
                else:
                    folded[k, rows_of(cut), :] = both
                    tile_copy(cut, k).start()
                if cut > 0 and pending:
                    forward(*pending.pop(0))
        pending += [(cut, k) for k in order[1:]]
    def mix_rows(e, cut, first, edges=None):
        for h in range(chunks):
            values = []
            for j in range(half):
                value = tuple(
                    full[
                        e * half + j, pl.ds((cut * parts + h * 2 + p) * cut_rows + first, group), :
                    ].astype(jnp.float32)
                    for p in range(2)
                )
                values.append(epoch_turn(value, j, epoch, epoch_count))
            done = dft(values + [None] * half, kept)
            if edges is not None:
                top = lax.broadcasted_iota(jnp.int32, (group, width), 0) == 0
                done = [
                    tuple(a + jnp.where(top, b, 0.0) for a, b in zip(part, edge))
                    for part, edge in zip(done, edges[h])
                ]
            for c, part in enumerate(done):
                for p in range(2):
                    row = pl.multiple_of(
                        p * band + e * rows_here + cut * cut_rows + first, group
                    )
                    mixed_ref[c, pl.ds(row, group), h * width : (h + 1) * width] = part[p].astype(
                        jnp.bfloat16
                    )

    def mix(e, cut):
        def step(i, carry):
            mix_rows(e, cut, pl.multiple_of(i * group, group))
            return carry

        lax.fori_loop(0, cut_rows // group, step, 0)

    def mix_crossed(cut):
        for j in range(1, epoch_count):

            def arrive(k, carry, j=j):
                epoch_copy(cut, k, j).wait_recv()
                return carry

            lax.fori_loop(0, half, arrive, 0)
            mix(lax.rem(epoch + epoch_count - j, epoch_count), cut)

    for cut in range(cuts):
        for item in pending:
            if item[0] == cut:
                forward(*item)
        mix(epoch, cut)
        if cut > 0:
            mix_crossed(cut - 1)
    mix_crossed(cuts - 1)

    edges = []
    for h in range(chunks):
        values = [None]
        for j in range(half):
            block = full[(epoch_count - 1) * half + j, cuts * parts * cut_rows :, :]
            block = block.astype(jnp.float32)
            value = tuple(block[h * 2 + p : h * 2 + p + 1] for p in range(2))
            values.append(epoch_turn(value, j + 1, epoch, epoch_count))
        edges.append(dft(values + [None] * (tile_count - half - 1), kept))
    mix_rows(0, 0, 0, edges)
    table_copy.wait()

    for cut in range(cuts):

        def finish(k, carry, cut=cut):
            tile_copy(cut, k).wait_send()
            return carry

        lax.fori_loop(1, half, finish, 0)

        def settle(k, carry, cut=cut):
            partner_copy(cut, k).wait_send()
            for j in range(1, epoch_count):
                epoch_copy(cut, k, j).wait_send()
            return carry

        lax.fori_loop(0, half, settle, 0)


def image_kernel(image_scale, mixed_ref, last_ref, rows_ref, cols_ref, out_ref, held, sem):
    kept = held.shape[0]
    tall = jnp.transpose(rows_ref[...]) * image_scale
    copies = [pltpu.make_async_copy(held.at[c], out_ref.at[c], sem.at[c]) for c in range(kept)]
    for c in range(kept):
        pixels = jnp.dot(last_ref[c], mixed_ref[c], preferred_element_type=jnp.float32)
        held[c] = pixels * tall[:, c : c + 1] * cols_ref[...]
        copies[c].start()
    for c in range(kept):
        copies[c].wait()


def turns(product, modulus):
    angles = (product % modulus) * (2.0 * math.pi / modulus)
    return np.cos(angles), np.sin(angles)


def make_tables(tile_count, block_len):
    grid_size = tile_count * block_len
    long_idx = np.arange(block_len)
    tile_idx = np.arange(tile_count)
    turn_cos, turn_sin = turns(tile_idx[:, None] * long_idx[None, :], grid_size)
    c, s = turns(long_idx[:, None] * long_idx[None, :], block_len)
    second = np.stack([np.stack([c, s], 1), np.stack([-s, c], 1)], 0)
    width = min(LANES, block_len)
    second = second.reshape(2 * block_len, 2, block_len // width, width)
    second = second.transpose(0, 2, 1, 3).reshape(2 * block_len, 2 * block_len)
    pixel = long_idx[None, :] * tile_count + tile_idx[:, None]
    c, s = turns(pixel[:, :, None] * long_idx[None, None, :], grid_size)
    last = np.concatenate([c, -s], -1)
    return (
        turn_cos.astype(np.float32),
        turn_sin.astype(np.float32),
        second.astype(jnp.bfloat16),
        last.astype(jnp.bfloat16),
    )


def hbm(count):
    return [pl.BlockSpec(memory_space=pltpu.HBM)] * count


def vmem(count):
    return [pl.BlockSpec(memory_space=pltpu.VMEM)] * count


def body(tables, owners, row_offsets, col_offsets, samples, coords, taper_rows, taper_cols):
    tile_count = lax.axis_size("tile")
    epoch_count = lax.axis_size("epoch")
    n_slots = owners.shape[1]
    n_samples = samples.shape[3]
    capacity = max(2, n_slots * 5 // (4 * tile_count))
    capacity += capacity % 2
    lane_step = max(8, 1 << (capacity - 1).bit_length())
    band = taper_cols.shape[0]
    width = min(LANES, band)
    half, kept = tile_count // 2, tile_count // epoch_count
    rows_here = band // epoch_count
    parts = 2 * (band // width)
    sizes = (tile_count, epoch_count, capacity, band)
    raw_rows = 2 * n_samples // LANES * capacity
    raw_shapes = [
        ((raw_rows, LANES), jnp.float32),
        ((-(-(raw_rows + FIELDS) // EDGE) * EDGE, LANES), jnp.bfloat16),
    ]
    spots = -(-tile_count // (LANES // lane_step)) * LANES

    tile_sems = pltpu.SemaphoreType.DMA((2, tile_count))
    epoch_sems = pltpu.SemaphoreType.DMA((2, (epoch_count - 1) * tile_count))
    pool, slot_list, weights = pl.pallas_call(
        functools.partial(grid_kernel, sizes),
        out_shape=[
            jax.ShapeDtypeStruct(
                (epoch_count * tile_count, capacity * SUB // 2, LANES), jnp.bfloat16
            ),
            jax.ShapeDtypeStruct((epoch_count, FIELDS, spots), jnp.int32),
            jax.ShapeDtypeStruct((epoch_count, FIELDS, LANES), jnp.float32),
        ],
        in_specs=hbm(5),
        out_specs=vmem(3),
        scratch_shapes=[
            *(
                pltpu.VMEM(array.shape, array.dtype)
                for array in (owners, row_offsets, col_offsets, coords, samples)
            ),
            pltpu.SemaphoreType.DMA((5,)),
            *(
                pltpu.VMEM((count, *shape), dtype)
                for count in (tile_count, epoch_count * tile_count)
                for shape, dtype in raw_shapes
            ),
            tile_sems,
            tile_sems,
            epoch_sems,
            epoch_sems,
        ],
        compiler_params=pltpu.CompilerParams(
            vmem_limit_bytes=VMEM_BYTES, collective_id=1, has_side_effects=True
        ),
        name="grid_slots",
    )(
        *(
            pltpu.with_memory_space_constraint(array, pltpu.HBM)
            for array in (owners, row_offsets, col_offsets, coords, samples)
        )
    )

    lane_blocks = tile_count * band // LANES
    acc = pl.pallas_call(
        functools.partial(place_kernel, tile_count),
        out_shape=jax.ShapeDtypeStruct(
            (2, lane_blocks + 1, rows_here + 2 * SUB, LANES), jnp.float32
        ),
        in_specs=[pl.BlockSpec(memory_space=pltpu.SMEM)] + vmem(2),
        out_specs=vmem(1)[0],
        compiler_params=pltpu.CompilerParams(vmem_limit_bytes=VMEM_BYTES),
        name="place_slots",
    )(slot_list, weights, pool)

    cuts = max(1, min(CUTS, rows_here // 16))
    block_shape = (parts * rows_here + EDGE, width)
    sems = [pltpu.SemaphoreType.DMA((cuts * half,))] * 4
    sems += [pltpu.SemaphoreType.DMA((cuts * (epoch_count - 1) * half,))] * 2
    mixed, last_here = pl.pallas_call(
        functools.partial(swap_kernel, (tile_count, epoch_count, band), cuts),
        out_shape=[
            jax.ShapeDtypeStruct((kept, 2 * band, band), jnp.bfloat16),
            jax.ShapeDtypeStruct((kept, band, 2 * band), jnp.bfloat16),
        ],
        in_specs=vmem(4) + hbm(1),
        out_specs=vmem(2),
        scratch_shapes=[
            pltpu.SemaphoreType.DMA((1,)),
            pltpu.VMEM((tile_count, rows_here + EDGE, 2 * band), jnp.bfloat16),
            pltpu.VMEM((half, *block_shape), jnp.bfloat16),
            pltpu.VMEM((half, *block_shape), jnp.bfloat16),
            pltpu.VMEM((half, *block_shape), jnp.bfloat16),
            pltpu.VMEM((epoch_count * half, *block_shape), jnp.bfloat16),
            *sems,
        ],
        compiler_params=pltpu.CompilerParams(
            vmem_limit_bytes=VMEM_BYTES, collective_id=0, has_side_effects=True
        ),
        name="swap_rows",
    )(acc, *(jnp.asarray(table) for table in tables))

    image_scale = math.sqrt(n_slots) / (64.0 * tile_count * math.sqrt(epoch_count))
    return pl.pallas_call(
        functools.partial(image_kernel, image_scale),
        out_shape=jax.ShapeDtypeStruct((kept, band, band), jnp.float32),
        in_specs=vmem(4),
        out_specs=hbm(1)[0],
        scratch_shapes=[
            pltpu.VMEM((kept, band, band), jnp.float32),
            pltpu.SemaphoreType.DMA((kept,)),
        ],
        compiler_params=pltpu.CompilerParams(vmem_limit_bytes=VMEM_BYTES),
        name="image_rows",
    )(mixed, last_here, taper_rows, taper_cols[None, :])


def solution(mesh):
    placed = (
        P("epoch", "tile"),
        P("epoch", "tile"),
        P("epoch", "tile"),
        P("epoch", "tile", None, None),
        P("epoch", "tile", None, None),
        P("epoch", None),
        P("tile"),
    )

    def whole(owners, row_offsets, col_offsets, samples, coords, taper_rows, taper_cols):
        tables = make_tables(mesh.shape["tile"], taper_cols.shape[0] // mesh.shape["tile"])
        return jax.shard_map(
            functools.partial(body, tables),
            mesh=mesh,
            in_specs=placed,
            out_specs=P("epoch", None, "tile"),
            check_vma=False,
        )(owners, row_offsets, col_offsets, samples, coords, taper_rows, taper_cols)

    return whole
```

profile of v0, /device:TPU:0, one launch (start us, length us, event | category | flops | bytes accessed | tf_op | source)
XLA Modules:
  0.0 68.5 jit_solution(10187677709204918800)
XLA Ops:
  0.0 26.6 %grid_slots.1 = (bf16[32,160,128]{2,1,0:T(8,128)(2,1)S(1)}, s32[2,8,256]{2,1,0:T(8,128)S(1)}, f32[2,8,128]{2,1,0:T(8,128)S(1)}) custom-call(s32[1,128]{1,0:T(1,128)} %refs_0_.1, s32[1,128]{1,0:T(1,128)} %refs_1_.1, s32[1,128]{1,0:T(1,128)} %refs_2_.1, f32[1,128,2,256]{3,2,1,0:T(2,128)} %refs_3_.1, bf16[1,128,2,256]{3,2,1,0:T(2,128)(2,1)} %refs_4_.1), custom_call_target="tpu_custom_call" | custom-call | tf_op jit(solution)/shard_map/grid_slots/pallas_call | solution.py:734
  26.6 0.0 copy-start
  26.6 0.0 copy-start.1
  26.6 0.0 copy-start.2
  26.7 0.0 copy-start.3
  26.7 3.3 %place_slots.1.acc_ref = f32[2,33,192,128]{3,2,1,0:T(8,128)S(1)} custom-call(s32[2,8,256]{2,1,0:T(8,128)S(1)} %get-tuple-element.10.list_ref, f32[2,8,128]{2,1,0:T(8,128)S(1)} %get-tuple-element.11.weight_ref, bf16[32,160,128]{2,1,0:T(8,128)(2,1)S(1)} %get-tuple-element.12.pool_ref), custom_call_target="tpu_custom_call" | custom-call | tf_op jit(solution)/shard_map/place_slots/pallas_call | solution.py:773
  29.9 0.0 copy-done
  29.9 0.0 copy-done.1
  29.9 0.0 copy-done.2
  30.0 0.0 copy-done.3
  30.0 0.0 copy-start.4
  30.0 0.0 copy-start.5
  30.0 36.8 %swap_rows.1 = (bf16[8,512,256]{2,1,0:T(8,128)(2,1)S(1)}, bf16[8,256,512]{2,1,0:T(8,128)(2,1)S(1)}) custom-call(f32[2,33,192,128]{3,2,1,0:T(8,128)S(1)} %place_slots.1.acc_ref, f32[16,256]{1,0:T(8,128)S(1)} %copy-done.3, f32[16,256]{1,0:T(8,128)S(1)} %copy-done.2, bf16[512,512]{1,0:T(8,128)(2,1)S(1)} %copy-done.1, bf16[16,256,512]{2,1,0:T(8,128)(2,1)S(1)} %copy-done), custom_call_target="tpu_custom_call" | custom-call | tf_op jit(solution)/shard_map/swap_rows/pallas_call | solution.py:788
  66.8 0.0 copy-done.4
  66.8 0.0 copy-done.5
  66.8 1.7 %image_rows.1 = f32[8,256,256]{2,1,0:T(8,128)} custom-call(bf16[8,512,256]{2,1,0:T(8,128)(2,1)S(1)} %get-tuple-element.13.mixed_ref, bf16[8,256,512]{2,1,0:T(8,128)(2,1)S(1)} %get-tuple-element.14.last_ref, f32[8,256]{1,0:T(8,128)S(1)} %copy-done.4, f32[1,256]{1,0:T(1,128)S(1)} %bitcast.1), custom_call_target="tpu_custom_call" | custom-call | tf_op jit(solution)/shard_map/image_rows/pallas_call | solution.py:812
Async XLA Ops:
  26.6 3.3 %copy-start = (bf16[16,256,512]{2,1,0:T(8,128)(2,1)S(1)}, bf16[16,256,512]{2,1,0:T(8,128)(2,1)}, u32[]{:S(2)}) copy-start(bf16[16,256,512]{2,1,0:T(8,128)(2,1)} %constant.11.clone.last_ref) | copy-start | bytes 12582916
  26.6 3.3 %copy-start.1 = (bf16[512,512]{1,0:T(8,128)(2,1)S(1)}, bf16[512,512]{1,0:T(8,128)(2,1)}, u32[]{:S(2)}) copy-start(bf16[512,512]{1,0:T(8,128)(2,1)} %constant.10.clone.second_ref) | copy-start | bytes 1572868
  26.6 3.3 %copy-start.2 = (f32[16,256]{1,0:T(8,128)S(1)}, f32[16,256]{1,0:T(8,128)}, u32[]{:S(2)}) copy-start(f32[16,256]{1,0:T(8,128)} %constant.9.clone.sin_ref) | copy-start | bytes 49156
  26.7 3.3 %copy-start.3 = (f32[16,256]{1,0:T(8,128)S(1)}, f32[16,256]{1,0:T(8,128)}, u32[]{:S(2)}) copy-start(f32[16,256]{1,0:T(8,128)} %constant.8.clone.cos_ref) | copy-start | bytes 49156
  30.0 36.8 %copy-start.4 = (f32[8,256]{1,0:T(8,128)S(1)}, f32[8,256]{1,0:T(8,128)}, u32[]{:S(2)}) copy-start(f32[8,256]{1,0:T(8,128)} %rows_ref.1) | copy-start | bytes 24580
  30.0 36.8 %copy-start.5 = (f32[256]{0:T(256)S(1)}, f32[256]{0:T(256)}, u32[]{:S(2)}) copy-start(f32[256]{0:T(256)} %param.17) | copy-start | bytes 3076
where the time goes:
time: 69.3 us; the launch traced here: 68.5 us
  Pallas kernels  68.4 us (99%)
    pallas_call x1, Pallas kernels, body(): pl.pallas_call(functools.partial(swap_kernel, (tile_count, epoch_count, b...  36.8 us
    pallas_call x1, Pallas kernels, body(): pl.pallas_call(functools.partial(grid_kernel, sizes), out_shape=[jax.Shap...  26.6 us
    pallas_call x1, Pallas kernels, body(): pl.pallas_call(functools.partial(place_kernel, tile_count), out_shape=jax...  3.26 us
    pallas_call x1, Pallas kernels, body(): pl.pallas_call(functools.partial(image_kernel, image_scale), out_shape=ja...  1.72 us

commit v1 on v0

--- a/solution.py
+++ b/solution.py
@@ -13,9 +13,9 @@
 LANES = 128
 EDGE = 16
 FIELDS = 8
-UNROLL = 8
-BEHIND = 3
-CUTS = 4
+UNROLL = 32
+BEHIND = 4
+CUTS = (32, 64, 32)
 VMEM_BYTES = 24 * 1024 * 1024
 MESH = pl.DeviceIdType.MESH
 
@@ -318,19 +318,30 @@
     field = lax.broadcasted_iota(jnp.int32, (FIELDS, spots), 0)
 
     def list_slots(j):
-        found, held = jnp.zeros((1, 1), jnp.float32), jnp.zeros((1, 1), jnp.float32)
-        gathered = jnp.zeros((EDGE, spots), jnp.float32)
+        held, wide, narrow = (jnp.zeros((1, 1), jnp.float32) for _ in range(3))
+        kinds = []
         for g in range(groups):
             total = jnp.zeros((info_rows, LANES), jnp.float32)
             for s in range(g * per_meta, min(tile_count, (g + 1) * per_meta)):
                 total += raw[1][j * tile_count + s, info:, :].astype(jnp.float32)
-            valid, row = total[0:1], total[1:2] - first_row
+            valid, row, start = total[0:1], total[1:2] - first_row, total[3:4]
             inside = (valid > 0) & (row > 0) & (row < rows_here + SUB)
-            mask = jnp.where(inside, 1.0, 0.0)
+            masks = [inside & (start > LANES - SUB), inside & (start <= LANES - SUB)]
+            flags = jnp.concatenate([jnp.where(mask, 1.0, 0.0) for mask in masks], 0)
             order = jnp.dot(
-                mask.astype(jnp.bfloat16), below, preferred_element_type=jnp.float32
+                flags.astype(jnp.bfloat16), below, preferred_element_type=jnp.float32
             )
-            chosen = spot == jnp.where(inside, order + found, -1.0)
+            kinds.append((total, row, masks, order, wide, narrow))
+            sums = jnp.sum(flags, 1, keepdims=True)
+            wide, narrow = wide + sums[0:1], narrow + sums[1:2]
+            held += jnp.sum(valid, 1, keepdims=True)
+        gathered = jnp.zeros((EDGE, spots), jnp.float32)
+        for g, (total, row, masks, order, wide_before, narrow_before) in enumerate(kinds):
+            chosen = spot == jnp.where(
+                masks[0],
+                order[0:1] + wide_before,
+                jnp.where(masks[1], order[1:2] + wide + narrow_before, -1.0),
+            )
             source = (g * per_meta + lanes // lane_step).astype(jnp.float32)
             place = (lanes % lane_step).astype(jnp.float32)
             rows = [source, row, total[2:3], total[3:4], place]
@@ -341,9 +352,8 @@
                 (((1,), (1,)), ((), ())),
                 preferred_element_type=jnp.float32,
             )
-            found += jnp.sum(mask, 1, keepdims=True)
-            held += jnp.sum(valid, 1, keepdims=True)
-        listed = jnp.where(field == FIELDS - 1, found, gathered[:FIELDS])
+        listed = jnp.where(field == FIELDS - 2, wide, gathered[:FIELDS])
+        listed = jnp.where(field == FIELDS - 1, wide + narrow, listed)
         list_ref[j] = listed.astype(jnp.int32)
         weight_ref[j] = jnp.broadcast_to(1.0 / jnp.maximum(held, 1.0), (FIELDS, LANES))
 
@@ -383,7 +393,7 @@
     for e in range(list_ref.shape[0]):
         weight = jnp.concatenate([weight_ref[e]] * (slot_rows // FIELDS), 0)
 
-        def per_batch(b, carry, e=e, weight=weight):
+        def per_batch(b, carry, e=e, weight=weight, blocks=2):
             placed = []
             for k in range(UNROLL):
                 at = b * UNROLL + k
@@ -400,21 +410,24 @@
                 windows = [
                     jnp.concatenate([jnp.where(mask, turned[i], 0.0) for i in (p, 2 + p)], 0)
                     for p in range(2)
-                    for mask in (near, far)
+                    for mask in (near, far)[:blocks]
                 ]
                 placed.append((row, block, windows))
             for row, block, windows in placed:
-                spots = [(p, block + h, pl.ds(row, SUB)) for p in range(2) for h in range(2)]
+                spots = [(p, block + h, pl.ds(row, SUB)) for p in range(2) for h in range(blocks)]
                 sums = [acc[spot] + window for spot, window in zip(spots, windows)]
                 for spot, total in zip(spots, sums):
                     acc[spot] = total
             return carry
 
-        lax.fori_loop(0, (list_ref[e, FIELDS - 1, 0] + UNROLL - 1) // UNROLL, per_batch, 0)
+        both = (list_ref[e, FIELDS - 2, 0] + UNROLL - 1) // UNROLL
+        last = (list_ref[e, FIELDS - 1, 0] + UNROLL - 1) // UNROLL
+        lax.fori_loop(0, both, per_batch, 0)
+        lax.fori_loop(both, last, functools.partial(per_batch, blocks=1), 0)
 
 
 def swap_kernel(
-    sizes, cuts, acc_ref, cos_ref, sin_ref, second_ref, last_ref, mixed_ref, here_ref, *scratch
+    sizes, spans, acc_ref, cos_ref, sin_ref, second_ref, last_ref, mixed_ref, here_ref, *scratch
 ):
     tile_count, epoch_count, band = sizes
     table_sem, scratch = scratch[0], scratch[1:]
@@ -429,12 +442,13 @@
     )
     table_copy.start()
     rows_here = band // epoch_count
-    cut_rows = rows_here // cuts
+    cuts = len(spans)
+    starts = [sum(spans[:cut]) for cut in range(cuts)]
     width = min(LANES, band)
     chunks = band // width
     parts = 2 * chunks
     lane_blocks = acc_ref.shape[1] - 1
-    group = min(16, cut_rows)
+    group = min(16, rows_here)
     batch = min(8, half)
 
     barrier = pltpu.get_barrier_semaphore()
@@ -452,7 +466,7 @@
 
     def rows_of(cut):
         edge = EDGE if cut == cuts - 1 else 0
-        return pl.ds(cut * parts * cut_rows, parts * cut_rows + edge)
+        return pl.ds(parts * starts[cut], parts * spans[cut] + edge)
 
     def partner_copy(cut, k):
         return pltpu.make_async_remote_copy(
@@ -513,8 +527,9 @@
     has_edge = jnp.where(epoch == epoch_count - 1, 1.0, 0.0)
 
     def sections(cut, tiles):
+        cut_rows = spans[cut]
         rows = cut_rows + (EDGE if cut == cuts - 1 else 0)
-        stack = [turned[tile, cut * cut_rows : cut * cut_rows + rows, :] for tile in tiles]
+        stack = [turned[tile, starts[cut] : starts[cut] + rows, :] for tile in tiles]
         moved = jnp.dot(
             jnp.concatenate(stack, 0), second_ref[...], preferred_element_type=jnp.float32
         )
@@ -539,21 +554,16 @@
 
     order = [0] + [k for pair in zip(range(1, half), range(half // 2, half)) for k in pair]
     order = order[: 1 + 2 * (half // 2 - 1)] + [half - 1] if half > 1 else [0]
-    pending = []
+    nearby = [k for k in order[1:] if 2 * k < half]
+    distant = [k for k in order[1:] if 2 * k >= half]
     for cut in range(cuts):
 
         def row_group(i, carry):
             transform(pl.multiple_of(i * group, group), group)
             return carry
 
-        if not pending:
-            steps = cut_rows // group
-            lax.fori_loop(cut * steps, (cut + 1) * steps, row_group, 0)
-        else:
-            for i in range(cut_rows // group):
-                transform(cut * cut_rows + i * group, group)
-                if pending:
-                    forward(*pending.pop(0))
+        first = starts[cut] // group
+        lax.fori_loop(first, first + spans[cut] // group, row_group, 0)
         if cut == cuts - 1:
             transform(rows_here, EDGE)
         if cut == 0:
@@ -577,16 +587,18 @@
                 else:
                     folded[k, rows_of(cut), :] = both
                     tile_copy(cut, k).start()
-                if cut > 0 and pending:
-                    forward(*pending.pop(0))
-        pending += [(cut, k) for k in order[1:]]
+        if cut > 0:
+            for k in nearby:
+                forward(cut - 1, k)
     def mix_rows(e, cut, first, edges=None):
         for h in range(chunks):
             values = []
             for j in range(half):
                 value = tuple(
                     full[
-                        e * half + j, pl.ds((cut * parts + h * 2 + p) * cut_rows + first, group), :
+                        e * half + j,
+                        pl.ds(parts * starts[cut] + (h * 2 + p) * spans[cut] + first, group),
+                        :,
                     ].astype(jnp.float32)
                     for p in range(2)
                 )
@@ -601,7 +613,7 @@
             for c, part in enumerate(done):
                 for p in range(2):
                     row = pl.multiple_of(
-                        p * band + e * rows_here + cut * cut_rows + first, group
+                        p * band + e * rows_here + starts[cut] + first, group
                     )
                     mixed_ref[c, pl.ds(row, group), h * width : (h + 1) * width] = part[p].astype(
                         jnp.bfloat16
@@ -612,7 +624,7 @@
             mix_rows(e, cut, pl.multiple_of(i * group, group))
             return carry
 
-        lax.fori_loop(0, cut_rows // group, step, 0)
+        lax.fori_loop(0, spans[cut] // group, step, 0)
 
     def mix_crossed(cut):
         for j in range(1, epoch_count):
@@ -625,9 +637,11 @@
             mix(lax.rem(epoch + epoch_count - j, epoch_count), cut)
 
     for cut in range(cuts):
-        for item in pending:
-            if item[0] == cut:
-                forward(*item)
+        for k in distant:
+            forward(cut, k)
+        if cut == 0:
+            for k in nearby:
+                forward(cuts - 1, k)
         mix(epoch, cut)
         if cut > 0:
             mix_crossed(cut - 1)
@@ -637,7 +651,7 @@
     for h in range(chunks):
         values = [None]
         for j in range(half):
-            block = full[(epoch_count - 1) * half + j, cuts * parts * cut_rows :, :]
+            block = full[(epoch_count - 1) * half + j, parts * rows_here :, :]
             block = block.astype(jnp.float32)
             value = tuple(block[h * 2 + p : h * 2 + p + 1] for p in range(2))
             values.append(epoch_turn(value, j + 1, epoch, epoch_count))
@@ -781,12 +795,14 @@
         name="place_slots",
     )(slot_list, weights, pool)
 
-    cuts = max(1, min(CUTS, rows_here // 16))
+    groups = [rows_here * share // 128 for share in CUTS]
+    spans = groups if all(span % 16 == 0 for span in groups) else [rows_here]
+    cuts = len(spans)
     block_shape = (parts * rows_here + EDGE, width)
     sems = [pltpu.SemaphoreType.DMA((cuts * half,))] * 4
     sems += [pltpu.SemaphoreType.DMA((cuts * (epoch_count - 1) * half,))] * 2
     mixed, last_here = pl.pallas_call(
-        functools.partial(swap_kernel, (tile_count, epoch_count, band), cuts),
+        functools.partial(swap_kernel, (tile_count, epoch_count, band), spans),
         out_shape=[
             jax.ShapeDtypeStruct((kept, 2 * band, band), jnp.bfloat16),
             jax.ShapeDtypeStruct((kept, band, 2 * band), jnp.bfloat16),

time: 69.3 us -> 67.4 us (0.973); the launches traced: 68.5 us -> 67.4 us
  Pallas kernels: 68.4 us -> 67.3 us
    pallas_call x1, Pallas kernels: 36.8 us -> 34.1 us  [body(): pl.pallas_call(functools.partial(swap_kernel, (tile_count, epoch_count, b...]
    pallas_call x1, Pallas kernels: 3.26 us -> 4.81 us  [body(): pl.pallas_call(functools.partial(place_kernel, tile_count), out_shape=jax...]
where the time goes in v1:
time: 67.4 us
  Pallas kernels  67.3 us (100%)
    pallas_call x1, Pallas kernels, body(): pl.pallas_call(functools.partial(swap_kernel, (tile_count, epoch_count, b...  34.1 us
    pallas_call x1, Pallas kernels, body(): pl.pallas_call(functools.partial(grid_kernel, sizes), out_shape=[jax.Shap...  26.6 us
    pallas_call x1, Pallas kernels, body(): pl.pallas_call(functools.partial(place_kernel, tile_count), out_shape=jax...  4.81 us
    pallas_call x1, Pallas kernels, body(): pl.pallas_call(functools.partial(image_kernel, image_scale), out_shape=ja...  1.72 us

profile of v1, /device:TPU:0, one launch (start us, length us, event | category | flops | bytes accessed | tf_op | source)
XLA Modules:
  0.0 67.4 jit_solution(4448296425291079128)
XLA Ops:
  0.0 26.6 %grid_slots.1 = (bf16[32,160,128]{2,1,0:T(8,128)(2,1)S(1)}, s32[2,8,256]{2,1,0:T(8,128)S(1)}, f32[2,8,128]{2,1,0:T(8,128)S(1)}) custom-call(s32[1,128]{1,0:T(1,128)} %refs_0_.1, s32[1,128]{1,0:T(1,128)} %refs_1_.1, s32[1,128]{1,0:T(1,128)} %refs_2_.1, f32[1,128,2,256]{3,2,1,0:T(2,128)} %refs_3_.1, bf16[1,128,2,256]{3,2,1,0:T(2,128)(2,1)} %refs_4_.1), custom_call_target="tpu_custom_call" | custom-call | tf_op jit(solution)/shard_map/grid_slots/pallas_call | solution.py:748
  26.6 0.0 copy-start
  26.6 0.0 copy-start.1
  26.6 0.0 copy-start.2
  26.7 0.0 copy-start.3
  26.7 4.8 %place_slots.1.acc_ref = f32[2,33,192,128]{3,2,1,0:T(8,128)S(1)} custom-call(s32[2,8,256]{2,1,0:T(8,128)S(1)} %get-tuple-element.10.list_ref, f32[2,8,128]{2,1,0:T(8,128)S(1)} %get-tuple-element.11.weight_ref, bf16[32,160,128]{2,1,0:T(8,128)(2,1)S(1)} %get-tuple-element.12.pool_ref), custom_call_target="tpu_custom_call" | custom-call | tf_op jit(solution)/shard_map/place_slots/pallas_call | solution.py:787
  31.5 0.0 copy-done
  31.5 0.0 copy-done.1
  31.5 0.0 copy-done.2
  31.5 0.0 copy-done.3
  31.5 0.0 copy-start.4
  31.5 0.0 copy-start.5
  31.5 34.1 %swap_rows.1 = (bf16[8,512,256]{2,1,0:T(8,128)(2,1)S(1)}, bf16[8,256,512]{2,1,0:T(8,128)(2,1)S(1)}) custom-call(f32[2,33,192,128]{3,2,1,0:T(8,128)S(1)} %place_slots.1.acc_ref, f32[16,256]{1,0:T(8,128)S(1)} %copy-done.3, f32[16,256]{1,0:T(8,128)S(1)} %copy-done.2, bf16[512,512]{1,0:T(8,128)(2,1)S(1)} %copy-done.1, bf16[16,256,512]{2,1,0:T(8,128)(2,1)S(1)} %copy-done), custom_call_target="tpu_custom_call" | custom-call | tf_op jit(solution)/shard_map/swap_rows/pallas_call | solution.py:804
  65.7 0.0 copy-done.4
  65.7 0.0 copy-done.5
  65.7 1.7 %image_rows.1 = f32[8,256,256]{2,1,0:T(8,128)} custom-call(bf16[8,512,256]{2,1,0:T(8,128)(2,1)S(1)} %get-tuple-element.13.mixed_ref, bf16[8,256,512]{2,1,0:T(8,128)(2,1)S(1)} %get-tuple-element.14.last_ref, f32[8,256]{1,0:T(8,128)S(1)} %copy-done.4, f32[1,256]{1,0:T(1,128)S(1)} %bitcast.1), custom_call_target="tpu_custom_call" | custom-call | tf_op jit(solution)/shard_map/image_rows/pallas_call | solution.py:828
Async XLA Ops:
  26.6 4.9 %copy-start = (bf16[16,256,512]{2,1,0:T(8,128)(2,1)S(1)}, bf16[16,256,512]{2,1,0:T(8,128)(2,1)}, u32[]{:S(2)}) copy-start(bf16[16,256,512]{2,1,0:T(8,128)(2,1)} %constant.11.clone.last_ref) | copy-start | bytes 12582916
  26.6 4.9 %copy-start.1 = (bf16[512,512]{1,0:T(8,128)(2,1)S(1)}, bf16[512,512]{1,0:T(8,128)(2,1)}, u32[]{:S(2)}) copy-start(bf16[512,512]{1,0:T(8,128)(2,1)} %constant.10.clone.second_ref) | copy-start | bytes 1572868
  26.6 4.9 %copy-start.2 = (f32[16,256]{1,0:T(8,128)S(1)}, f32[16,256]{1,0:T(8,128)}, u32[]{:S(2)}) copy-start(f32[16,256]{1,0:T(8,128)} %constant.9.clone.sin_ref) | copy-start | bytes 49156
  26.7 4.9 %copy-start.3 = (f32[16,256]{1,0:T(8,128)S(1)}, f32[16,256]{1,0:T(8,128)}, u32[]{:S(2)}) copy-start(f32[16,256]{1,0:T(8,128)} %constant.8.clone.cos_ref) | copy-start | bytes 49156
  31.5 34.2 %copy-start.4 = (f32[8,256]{1,0:T(8,128)S(1)}, f32[8,256]{1,0:T(8,128)}, u32[]{:S(2)}) copy-start(f32[8,256]{1,0:T(8,128)} %rows_ref.1) | copy-start | bytes 24580
  31.5 34.2 %copy-start.5 = (f32[256]{0:T(256)S(1)}, f32[256]{0:T(256)}, u32[]{:S(2)}) copy-start(f32[256]{0:T(256)} %param.17) | copy-start | bytes 3076

commit v2 on v1

--- a/solution.py
+++ b/solution.py
@@ -97,14 +97,6 @@
         x, y = lax.rem(a // (1 << bit), 2), lax.rem(b // (1 << bit), 2)
         total += (x + y - 2 * x * y) * (1 << bit)
     return total
-
-
-def near_and_far(i, count):
-    return jnp.where(
-        i == count - 2,
-        count - 1,
-        jnp.where(lax.rem(i, 2) == 0, 1 + i // 2, count // 2 + i // 2),
-    )
 
 
 def grid_kernel(
@@ -227,12 +219,12 @@
             for part in range(2)
         ]
 
-    def send(i, carry):
-        for copy in tile_copies(near_and_far(i, tile_count)):
+    def send(k, carry):
+        for copy in tile_copies(k):
             copy.start()
         return carry
 
-    lax.fori_loop(0, tile_count - 1, send, 0)
+    lax.fori_loop(1, tile_count, send, 0)
     for part in range(2):
         raw[part][me] = packed[part][me]
     for j in range(1, epoch_count):
@@ -272,8 +264,7 @@
 
     make(me)
 
-    def take(i):
-        k = near_and_far(i, tile_count)
+    def take(k):
         for copy in tile_copies(k):
             copy.wait_recv()
         for j in range(1, epoch_count):
@@ -281,8 +272,7 @@
                 copy.start()
         make(exclusive(me, k, tile_count))
 
-    def take_crossed(i):
-        k = jnp.where(i == 0, 0, near_and_far(i - 1, tile_count))
+    def take_crossed(k):
         for j in range(1, epoch_count):
             for copy in epoch_copies(k, j):
                 copy.wait_recv()
@@ -290,21 +280,21 @@
 
     behind = min(BEHIND, tile_count - 1)
 
-    def ahead(i, carry):
-        take(i)
+    def ahead(k, carry):
+        take(k)
         return carry
 
-    def both(i, carry):
-        take(i)
-        take_crossed(i - behind)
+    def both(k, carry):
+        take(k)
+        take_crossed(k - 1 - behind)
         return carry
 
-    def crossed(i, carry):
-        take_crossed(i)
+    def crossed(k, carry):
+        take_crossed(k)
         return carry
 
-    lax.fori_loop(0, behind, ahead, 0)
-    lax.fori_loop(behind, tile_count - 1, both, 0)
+    lax.fori_loop(1, 1 + behind, ahead, 0)
+    lax.fori_loop(1 + behind, tile_count, both, 0)
 
     rows_here = band // epoch_count
     first_row = (epoch * rows_here - SUB).astype(jnp.float32)
@@ -552,8 +542,7 @@
         for j in range(1, epoch_count):
             epoch_copy(cut, k, j).start()
 
-    order = [0] + [k for pair in zip(range(1, half), range(half // 2, half)) for k in pair]
-    order = order[: 1 + 2 * (half // 2 - 1)] + [half - 1] if half > 1 else [0]
+    order = list(range(half))
     nearby = [k for k in order[1:] if 2 * k < half]
     distant = [k for k in order[1:] if 2 * k >= half]
     for cut in range(cuts):

time: 67.4 us -> 65.8 us (0.976)
  Pallas kernels: 67.3 us -> 65.3 us
    pallas_call x1, Pallas kernels: 26.6 us -> 24.6 us  [body(): pl.pallas_call(functools.partial(grid_kernel, sizes), out_shape=[jax.Shap...]
    pallas_call x1, Pallas kernels: 34.1 us -> 35.4 us  [body(): pl.pallas_call(functools.partial(swap_kernel, (tile_count, epoch_count, b...]
    pallas_call x1, Pallas kernels: 4.81 us -> 3.65 us  [body(): pl.pallas_call(functools.partial(place_kernel, tile_count), out_shape=jax...]
where the time goes in v2:
time: 65.8 us; the launch traced here: 65.5 us
  Pallas kernels  65.3 us (99%)
    pallas_call x1, Pallas kernels, body(): pl.pallas_call(functools.partial(swap_kernel, (tile_count, epoch_count, b...  35.4 us
    pallas_call x1, Pallas kernels, body(): pl.pallas_call(functools.partial(grid_kernel, sizes), out_shape=[jax.Shap...  24.6 us
    pallas_call x1, Pallas kernels, body(): pl.pallas_call(functools.partial(place_kernel, tile_count), out_shape=jax...  3.65 us
    pallas_call x1, Pallas kernels, body(): pl.pallas_call(functools.partial(image_kernel, image_scale), out_shape=ja...  1.72 us

profile of v2, /device:TPU:0, one launch (start us, length us, event | category | flops | bytes accessed | tf_op | source)
XLA Modules:
  0.0 65.5 jit_solution(5361315727459196627)
XLA Ops:
  0.0 24.6 %grid_slots.1 = (bf16[32,160,128]{2,1,0:T(8,128)(2,1)S(1)}, s32[2,8,256]{2,1,0:T(8,128)S(1)}, f32[2,8,128]{2,1,0:T(8,128)S(1)}) custom-call(s32[1,128]{1,0:T(1,128)} %refs_0_.1, s32[1,128]{1,0:T(1,128)} %refs_1_.1, s32[1,128]{1,0:T(1,128)} %refs_2_.1, f32[1,128,2,256]{3,2,1,0:T(2,128)} %refs_3_.1, bf16[1,128,2,256]{3,2,1,0:T(2,128)(2,1)} %refs_4_.1), custom_call_target="tpu_custom_call" | custom-call | tf_op jit(solution)/shard_map/grid_slots/pallas_call | solution.py:737
  24.6 0.0 copy-start
  24.6 0.0 copy-start.1
  24.6 0.0 copy-start.2
  24.6 0.0 copy-start.3
  24.6 3.7 %place_slots.1.acc_ref = f32[2,33,192,128]{3,2,1,0:T(8,128)S(1)} custom-call(s32[2,8,256]{2,1,0:T(8,128)S(1)} %get-tuple-element.10.list_ref, f32[2,8,128]{2,1,0:T(8,128)S(1)} %get-tuple-element.11.weight_ref, bf16[32,160,128]{2,1,0:T(8,128)(2,1)S(1)} %get-tuple-element.12.pool_ref), custom_call_target="tpu_custom_call" | custom-call | tf_op jit(solution)/shard_map/place_slots/pallas_call | solution.py:776
  28.3 0.0 copy-done
  28.3 0.0 copy-done.1
  28.3 0.0 copy-done.2
  28.3 0.0 copy-done.3
  28.3 0.0 copy-start.4
  28.3 0.0 copy-start.5
  28.4 35.4 %swap_rows.1 = (bf16[8,512,256]{2,1,0:T(8,128)(2,1)S(1)}, bf16[8,256,512]{2,1,0:T(8,128)(2,1)S(1)}) custom-call(f32[2,33,192,128]{3,2,1,0:T(8,128)S(1)} %place_slots.1.acc_ref, f32[16,256]{1,0:T(8,128)S(1)} %copy-done.3, f32[16,256]{1,0:T(8,128)S(1)} %copy-done.2, bf16[512,512]{1,0:T(8,128)(2,1)S(1)} %copy-done.1, bf16[16,256,512]{2,1,0:T(8,128)(2,1)S(1)} %copy-done), custom_call_target="tpu_custom_call" | custom-call | tf_op jit(solution)/shard_map/swap_rows/pallas_call | solution.py:793
  63.8 0.0 copy-done.4
  63.8 0.0 copy-done.5
  63.8 1.7 %image_rows.1 = f32[8,256,256]{2,1,0:T(8,128)} custom-call(bf16[8,512,256]{2,1,0:T(8,128)(2,1)S(1)} %get-tuple-element.13.mixed_ref, bf16[8,256,512]{2,1,0:T(8,128)(2,1)S(1)} %get-tuple-element.14.last_ref, f32[8,256]{1,0:T(8,128)S(1)} %copy-done.4, f32[1,256]{1,0:T(1,128)S(1)} %bitcast.1), custom_call_target="tpu_custom_call" | custom-call | tf_op jit(solution)/shard_map/image_rows/pallas_call | solution.py:817
Async XLA Ops:
  24.6 3.7 %copy-start = (bf16[16,256,512]{2,1,0:T(8,128)(2,1)S(1)}, bf16[16,256,512]{2,1,0:T(8,128)(2,1)}, u32[]{:S(2)}) copy-start(bf16[16,256,512]{2,1,0:T(8,128)(2,1)} %constant.11.clone.last_ref) | copy-start | bytes 12582916
  24.6 3.7 %copy-start.1 = (bf16[512,512]{1,0:T(8,128)(2,1)S(1)}, bf16[512,512]{1,0:T(8,128)(2,1)}, u32[]{:S(2)}) copy-start(bf16[512,512]{1,0:T(8,128)(2,1)} %constant.10.clone.second_ref) | copy-start | bytes 1572868
  24.6 3.7 %copy-start.2 = (f32[16,256]{1,0:T(8,128)S(1)}, f32[16,256]{1,0:T(8,128)}, u32[]{:S(2)}) copy-start(f32[16,256]{1,0:T(8,128)} %constant.9.clone.sin_ref) | copy-start | bytes 49156
  24.6 3.7 %copy-start.3 = (f32[16,256]{1,0:T(8,128)S(1)}, f32[16,256]{1,0:T(8,128)}, u32[]{:S(2)}) copy-start(f32[16,256]{1,0:T(8,128)} %constant.8.clone.cos_ref) | copy-start | bytes 49156
  28.3 35.4 %copy-start.4 = (f32[8,256]{1,0:T(8,128)S(1)}, f32[8,256]{1,0:T(8,128)}, u32[]{:S(2)}) copy-start(f32[8,256]{1,0:T(8,128)} %rows_ref.1) | copy-start | bytes 24580
  28.3 35.4 %copy-start.5 = (f32[256]{0:T(256)S(1)}, f32[256]{0:T(256)}, u32[]{:S(2)}) copy-start(f32[256]{0:T(256)} %param.17) | copy-start | bytes 3076
